TPU v7x, 1024 devices: a whole 4x8x16 slice. The times are simulated.
1024 devices in a mesh: blk: 32 (over x_lo, z), rep: 32 (over x_hi, y, core).
Axes of the slice: x: 4 (x_hi: 2, x_lo: 2; x = x_hi * 2 + x_lo), y: 8, z: 16, core: 2. Of those that a mesh axis runs over, the one named last changes fastest.
Arguments:
- amps: bfloat16 [1024, 65536], P(None, ('rep', 'blk')), may hold values from -6 to 6
- amp_tiles: int32 [1024, 1024], P(None, ('rep', 'blk')), may hold values 0 or 1
- ints: bfloat16 [65536, 16384], P('rep', 'blk'), may hold values from -0.0234375 to 0.0234375
- int_tiles: int32 [1024, 256], P('rep', 'blk'), may hold values from 0 to 1, as said below
Outputs:
- ladder: float32 [1024, 16384], P('rep', 'blk')
Inputs may be any that keep to these rules, and one draw needn't show every extreme that they name: `int_tiles`: each entry is 0 or 1; the share of kept tiles differs from one residual column tile to another.
All inputs are finite; a program needn't handle non-finite values. No bound on the sum of `amp_tiles` on one device may be relied on, other than what follows from the above.
Results may differ from a plain program's by a relative error of at most 0.0003.
Values may be sent and summed in bfloat16 or wider, within the bound.
No kernel may reach another device: no remote copies, remote signals or barrier semaphores. Data moves between devices by JAX's collectives and lax.ppermute only.
A program may use at most 32 MiB of HBM per device.

v0:
```python
import jax
import jax.numpy as jnp
from jax import lax
from jax.sharding import PartitionSpec as P

TILE = 64


def per_device(amps, amp_tiles, ints, int_tiles):
    amp_mask = jnp.repeat(amp_tiles, TILE, axis=1)
    amp_full = jnp.where(amp_mask > 0, amps, jnp.zeros_like(amps))
    tile_rows = int_tiles.shape[0]
    tile_cols = int_tiles.shape[1]
    shaped_ints = ints.reshape(tile_rows, TILE, tile_cols, TILE)
    keep_flags = (int_tiles > 0)[:, None, :, None]
    int_full = jnp.where(keep_flags, shaped_ints, jnp.zeros_like(shaped_ints)).reshape(ints.shape)
    gathered = lax.all_gather(amp_full, "blk", axis=1, tiled=True)
    partial_value = jnp.dot(gathered, int_full, preferred_element_type=jnp.float32)
    return lax.psum_scatter(partial_value, "rep", scatter_dimension=0, tiled=True)


def solution(mesh):
    return jax.shard_map(
        per_device,
        mesh=mesh,
        in_specs=(
            P(None, ("rep", "blk")),
            P(None, ("rep", "blk")),
            P("rep", "blk"),
            P("rep", "blk"),
        ),
        out_specs=P("rep", "blk"),
        check_vma=False,
    )
```

profile of v0, /device:TPU:16, one launch (start us, length us, event | category | flops | bytes accessed | tf_op | source)
XLA Modules:
  0.0 309.6 jit_solution(14829134577408476404)
XLA Ops:
  6.5 0.0 all-gather.2.cloned.1.call-start
  6.5 0.7 compare_reduce_fusion
  7.2 1.6 broadcast_select_fusion
  8.8 0.0 all-gather.2.cloned.1.call-update
  8.8 0.0 reduce-scatter.2.cloned.1.call-start
  8.9 0.7 broadcast_compare_fusion
  9.6 0.1 copy.5
  9.7 0.6 broadcast_in_dim.19
  10.3 4.0 %broadcast_in_dim.20 = pred[2048,512]{1,0:T(32,128)(4,1)S(1)} reshape(pred[32,64,8,64]{3,2,1,0:T(8,128)(4,1)S(1)} %broadcast_in_dim.19) | data formatting | bytes 2097152 | tf_op jit(solution)/shard_map/jit(_where)/broadcast_in_dim | solution.py:16
  14.3 145.0 %all-gather.2.cloned.1.call-done = bf16[1024,2048]{0,1:T(8,128)(2,1)} async-done(((bf16[1024,64]{0,1:T(8,128)(2,1)}), bf16[1024,2048]{0,1:T(8,128)(2,1)}) %all-gather.2.cloned.1.call-update) | async-done | bytes 4194320 | tf_op jit(solution)/shard_map/all_gather | solution.py:17
  159.3 6.6 %fusion = f32[1024,512]{1,0:T(8,128)} fusion(bf16[1024,2048]{0,1:T(8,128)(2,1)} %all-gather.2.cloned.1.call-done, pred[2048,512]{1,0:T(32,128)(4,1)S(1)} %broadcast_in_dim.20, bf16[2048,512]{1,0:T(8,128)(2,1)} %param.6), kind=kOutput, calls=%fused_computation | convolution fusion | flops 2148532224 | bytes 9437184 | tf_op jit(solution)/shard_map/dot_general | solution.py:18
  165.9 0.0 reduce-scatter.2.cloned.1.call-update
  165.9 136.9 %reduce-scatter.2.cloned.1.call-done = f32[32,512]{1,0:T(8,128)} async-done(((f32[1024,512]{1,0:T(8,128)}), f32[32,512]{1,0:T(8,128)}) %reduce-scatter.2.cloned.1.call-update) | async-done | bytes 65552 | tf_op jit(solution)/shard_map/reduce_scatter | solution.py:19
Async XLA Ops:
  6.5 152.8 %all-gather.2.cloned.1.call-start = ((), (), s32[]{:S(2)}) async-start(), calls=%async_computation.1 | async-start | bytes 4325376 | tf_op jit(solution)/shard_map/all_gather | solution.py:17
  8.8 293.9 %reduce-scatter.2.cloned.1.call-start = ((), (), s32[]{:S(2)}) async-start(), calls=%async_computation.2 | async-start | bytes 2162688 | tf_op jit(solution)/shard_map/reduce_scatter | solution.py:19
Sparse Core Ops, SparseCore 0:
  10.0 149.2 all-gather.1
  166.0 136.6 reduce-scatter.1
where the time goes:
time: 310 us
  waiting for transfers between devices  282 us (91%)
  between operations  13.4 us (4%)
  matrix products  6.57 us (2%)
  local copies, waits for them, and re-layouts  4.69 us (2%)
    all_gather x1, waiting for transfers between devices, per_device(): gathered = lax.all_gather(amp_full, 'blk', axis=1, tiled=True)  145 us
    reduce_scatter x1, waiting for transfers between devices, per_device(): lax.psum_scatter(partial_value, 'rep', scatter_dimension=0, tiled=True)  137 us
    dot_general x1, matrix products, per_device(): jnp.dot(gathered, int_full, preferred_element_type=jnp.float32)  6.57 us
  transfers between devices with their start and end apart: 2, of which 2 were waited for; matrix products, arithmetic and copies ran while one was open for 2% of the time, Pallas kernels for 0%

commit v1 on v0

v1 whole, which is shorter than its diff:
```python
import jax
import jax.numpy as jnp
from jax import lax
from jax.sharding import PartitionSpec as P

TILE = 64
Z = 16
SHIFT = 13
SPAN = 29
LEAST = -26
ZERO_MARK = 65504.0


def power_below(t):
    power = jnp.full_like(t, 2.0**-13)
    for step in (16, 8, 4, 2, 1):
        higher = power * 2.0**step
        power = jnp.where(t >= higher, higher, power)
    return power


def encode(x):
    value = x.astype(jnp.float32)
    size = jnp.abs(value)
    level = jnp.zeros(x.shape, jnp.int32)
    for j in range(4):
        level += ((size < 2.0 ** (LEAST - SPAN * j)) & (size > 0)).astype(jnp.int32)
    rare = jnp.any(level > 0)
    raised = value
    for j in range(1, 5):
        raised = jnp.where(level == j, value * 2.0 ** (SPAN * j), raised)
    raised = raised * 2.0**SHIFT
    low = jnp.where(level == 4, -1, level)
    first = (lax.broadcasted_iota(jnp.int32, x.shape, 0) + lax.broadcasted_iota(jnp.int32, x.shape, 1)) == 0
    marked = first & rare
    low = jnp.where(marked & (level == 0), -2, low)
    bits = low.astype(jnp.float32) * power_below(jnp.abs(raised)) * 2.0**-10
    code = jnp.where(raised < 0, raised - bits, raised + bits)
    code = jnp.where(size > 0, code, jnp.where(marked, ZERO_MARK, 0.0))
    return code.astype(jnp.float16)


def decode_rare(code):
    h = code.astype(jnp.float32)
    t = h.astype(jnp.bfloat16).astype(jnp.float32)
    low = (jnp.abs(h) - jnp.abs(t)) * 2.0**10 / power_below(jnp.abs(t))
    value = t
    for level, bits in ((1, 1.0), (2, 2.0), (3, 3.0), (4, -1.0)):
        value = jnp.where(low == bits, t * 2.0 ** (-SPAN * level), value)
    value = jnp.where(h == ZERO_MARK, 0.0, value)
    return value.astype(jnp.bfloat16)


def per_device(amps, amp_tiles, ints, int_tiles):
    x_lo = lax.axis_index("blk") // Z
    core = lax.axis_index("rep") % 2
    rows = amps.shape[0]
    cols = ints.shape[1]

    own = encode(jnp.where(amp_tiles.T > 0, amps.T, jnp.zeros_like(amps.T)))
    other = lax.ppermute(own, "blk", [(b, b ^ Z) for b in range(2 * Z)])
    pair = jnp.where(x_lo == 0, jnp.concatenate([own, other]), jnp.concatenate([other, own]))
    rings = [[h * Z + z for z in range(Z)] for h in range(2)]
    codes = lax.all_gather(pair[None], "blk", axis=0, tiled=True, axis_index_groups=rings)

    flags = jnp.repeat((int_tiles > 0).reshape(2, Z, -1), TILE, axis=2)
    blocks = ints.reshape(2, Z, TILE, cols)
    kept = jnp.where(flags[:, :, None, :], blocks, jnp.zeros_like(blocks))
    kept = kept.transpose(1, 0, 2, 3).reshape(-1, cols)
    kept = lax.optimization_barrier(kept)

    heads = codes.reshape(2 * Z, TILE, rows)[:, 0, :1].astype(jnp.float32)
    rare = jnp.any(heads != heads.astype(jnp.bfloat16).astype(jnp.float32))

    def product(table):
        return lax.dot_general(
            table.reshape(-1, rows), kept, (((0,), (0,)), ((), ())), preferred_element_type=jnp.float32
        )

    total = lax.cond(
        rare,
        lambda c: product(decode_rare(c)),
        lambda c: product(c.astype(jnp.bfloat16)),
        codes,
    )

    parts = total.reshape(16, 2, -1, cols)
    mine = lax.dynamic_index_in_dim(parts, core, 1, keepdims=False)
    theirs = lax.dynamic_index_in_dim(parts, 1 - core, 1, keepdims=False)
    mine = mine + lax.ppermute(theirs, "rep", [(r, r ^ 1) for r in range(32)])
    peers = [[c + 2 * i for i in range(16)] for c in range(2)]
    shares = lax.all_to_all(mine, "rep", 0, 0, tiled=True, axis_index_groups=peers)
    return jnp.sum(shares, axis=0) * 2.0**-SHIFT


def solution(mesh):
    return jax.shard_map(
        per_device,
        mesh=mesh,
        in_specs=(
            P(None, ("rep", "blk")),
            P(None, ("rep", "blk")),
            P("rep", "blk"),
            P("rep", "blk"),
        ),
        out_specs=P("rep", "blk"),
        check_vma=False,
    )
```

time: 310 us -> 150 us (0.48)
  the two profiles are of different devices: /device:TPU:16 before, /device:TPU:64 now
where the time goes in v1:
time: 150 us
  blocking collectives  111 us (74%)
  other arithmetic  15.7 us (10%)
  local copies, waits for them, and re-layouts  11.8 us (8%)
  starting transfers between devices  5.32 us (4%)
  waiting for transfers between devices  2.75 us (2%)
  matrix products  2.34 us (2%)
    all_gather x1, blocking collectives, per_device(): lax.all_gather(pair[None], 'blk', axis=0, tiled=True, axis_index_groups=r...  73 us
    all_to_all x1, blocking collectives, per_device(): lax.all_to_all(mine, 'rep', 0, 0, tiled=True, axis_index_groups=peers)  37.7 us
    another operation x1, local copies, waits for them, and re-layouts  7.28 us
    ppermute x1, starting transfers between devices, per_device(): other = lax.ppermute(own, 'blk', [(b, b ^ Z) for b in range(2 * Z)])  3.4 us
    select_n x1, other arithmetic, per_device(): kept = jnp.where(flags[:, :, None, :], blocks, jnp.zeros_like(blocks))  3.18 us
  transfers between devices with their start and end apart: 2, of which 1 were waited for; matrix products, arithmetic and copies ran while one was open for 4% of the time, Pallas kernels for 0%

profile of v1, /device:TPU:64, one launch (start us, length us, event | category | flops | bytes accessed | tf_op | source)
XLA Modules:
  0.0 149.6 jit_solution(9794107256068518667)
XLA Ops:
  0.0 0.0 copy-start.3
  0.0 0.7 compare_reduce_fusion.1
  0.7 1.7 %compare_reduce_fusion = pred[]{:T(512)} fusion(bf16[1024,64]{0,1:T(8,128)(2,1)} %param.6, pred[1024]{0:T(1024)(128)(4,1)S(1)} %compare_reduce_fusion.1), kind=kLoop, calls=%fused_computation.63 | loop fusion | flops 1376255 | bytes 132097 | tf_op jit(solution)/shard_map/reduce_or | solution.py:28
  2.5 2.1 %select_convert_fusion = f16[64,1024]{1,0:T(8,128)(2,1)S(1)} fusion(pred[]{:T(512)} %compare_reduce_fusion, bf16[1024,64]{0,1:T(8,128)(2,1)} %param.6, pred[1024]{0:T(1024)(128)(4,1)S(1)} %compare_reduce_fusion.1), kind=kLoop, calls=%fused_computation.55 | loop fusion | flops 4194304 | bytes 263169 | tf_op jit(solution)/shard_map/convert_element_type | solution.py:40
  4.5 3.4 %collective-permute-start = (f16[64,1024]{1,0:T(8,128)(2,1)S(1)}, f16[64,1024]{1,0:T(8,128)(2,1)S(1)}, u32[]{:S(2)}, u32[]{:S(2)}) collective-permute-start(f16[64,1024]{1,0:T(8,128)(2,1)S(1)} %select_convert_fusion), channel_id=1, source_target_pairs={{0,512},{32,544},{64,576},{96,608},{128,640},{160,672},{192,704},{... | collective-permute-start | bytes 393224 | tf_op jit(solution)/shard_map/ppermute | solution.py:61
  8.0 0.7 broadcast_compare_fusion
  8.7 0.1 copy.26
  8.7 0.1 broadcast_in_dim.54
  8.9 0.1 broadcast_in_dim.55
  9.0 3.2 %copy_select_fusion = bf16[2,16,64,512]{3,2,0,1:T(8,128)(2,1)} fusion(bf16[2,16,64,512]{3,2,1,0:T(8,128)(2,1)} %bitcast.107, pred[2,16,512]{2,0,1:T(4,128)(4,1)S(1)} %copy.20), kind=kLoop, calls=%fused_computation.28 | loop fusion | flops 1048576 | bytes 4210688 | tf_op jit(solution)/shard_map/jit(_where)/select_n | solution.py:68
  12.2 0.0 copy-done.3
  12.2 1.2 fusion.34
  13.4 0.0 collective-permute-done
  13.4 0.1 maximum_select_fusion
  13.5 73.0 %all-gather.1 = f16[16,128,1024]{2,1,0:T(8,128)(2,1)S(1)} all-gather(f16[1,128,1024]{2,1,0:T(8,128)(2,1)S(1)} %maximum_select_fusion), channel_id=1, replica_groups={{0,32,64,96,128,160,192,224,256,288,320,352,384,416,448,480},{512,544,5..., dimensions={0}, use_global_device_ids=true | all-gather | bytes 4456448 | tf_op jit(solution)/shard_map/all_gather | solution.py:64
  86.5 0.0 copy-start
  86.5 1.9 %copy-done = f16[16,128,1024]{2,1,0:T(8,128)(2,1)} copy-done((f16[16,128,1024]{2,1,0:T(8,128)(2,1)}, f16[16,128,1024]{2,1,0:T(8,128)(2,1)S(1)}, u32[]{:S(2)}) %copy-start) | copy-done | bytes 4194328
  88.5 0.3 fusion.30
  88.8 0.6 compare_reduce_fusion.2
  90.1 14.9 %conditional.1 = (f32[16,2,32,512]{3,2,1,0:T(8,128)S(1)}) conditional(s32[]{:T(128)} %convert_element_type.90, (f16[16,128,1024]{2,1,0:T(8,128)(2,1)}, bf16[2048,512]{1,0:T(8,128)(2,1)}) %tuple.24, (f16[16,128,1024]{2,1,0:T(8,128)(2,1)}, bf16[2048,512]{1,0:T(8,128)(2,1)}) %tuple.25), branch_computations={%region_2.3_spmd, %region_3.4_spmd} | conditional | flops 2225078272 | bytes 41943076 | solution.py:80
  90.1 7.3 %copy.22 = f16[16,128,1024]{1,0,2:T(8,128)(2,1)} copy(f16[16,128,1024]{2,1,0:T(8,128)(2,1)} %get-tuple-element.29) | data formatting | bytes 8388608 | tf_op jit(solution)/shard_map
  97.4 2.9 %convert_element_type.60 = bf16[16,128,1024]{1,0,2:T(8,128)(2,1)S(1)} convert(f16[16,128,1024]{1,0,2:T(8,128)(2,1)} %copy.22) | non-fusion elementwise | flops 2097152 | bytes 8388608 | tf_op jit(solution)/shard_map/cond/branch_0_fun/convert_element_type | solution.py:83
  100.3 0.0 copy-start.1
  100.3 2.2 %copy.32 = bf16[128,8,16,128]{3,1,2,0:T(8,128)(2,1)S(1)} copy(bf16[128,8,16,128]{3,2,1,0:T(8,128)(2,1)S(1)} %bitcast.103) | data formatting | bytes 8388608 | tf_op jit(solution)/shard_map/cond
  102.4 0.0 copy-done.1
  102.5 2.3 %fusion = f32[16,2,32,512]{3,2,1,0:T(8,128)S(1)} fusion(bf16[16,2,32,2048]{3,2,1,0:T(8,128)(2,1)S(1)} %bitcast.105, bf16[2048,512]{1,0:T(8,128)(2,1)S(1)} %copy-done.1), kind=kOutput, calls=%fused_computation.1 | convolution fusion | flops 2147483648 | bytes 8388608 | tf_op jit(solution)/shard_map/cond/branch_0_fun/dot_general | solution.py:76
  105.0 0.1 dynamic-slice_bitcast_fusion
  105.1 1.9 %collective-permute-start.1 = (f32[16,32,512]{2,1,0:T(8,128)S(1)}, f32[16,32,512]{2,1,0:T(8,128)}, u32[]{:S(2)}, u32[]{:S(2)}) collective-permute-start(f32[16,32,512]{2,1,0:T(8,128)S(1)} %dynamic-slice_bitcast_fusion), channel_id=1, source_target_pairs={{0,1},{1,0},{2,3},{3,2},{4,5},{5,4},{6,7},{7,6},{8,9},{9,8},{10,11... | collective-permute-start | bytes 3145736 | tf_op jit(solution)/shard_map/ppermute | solution.py:90
  107.0 2.8 %collective-permute-done.1 = f32[16,32,512]{2,1,0:T(8,128)} collective-permute-done((f32[16,32,512]{2,1,0:T(8,128)S(1)}, f32[16,32,512]{2,1,0:T(8,128)}, u32[]{:S(2)}, u32[]{:S(2)}) %collective-permute-start.1) | collective-permute-done | bytes 1048608 | tf_op jit(solution)/shard_map/ppermute | solution.py:90
  109.8 1.4 bitcast_add_fusion
  111.2 37.7 %all_to_all.5 = f32[16,32,512]{2,1,0:T(8,128)S(1)} all-to-all(f32[16,32,512]{2,1,0:T(8,128)S(1)} %bitcast_add_fusion), channel_id=1, replica_groups={{0,2,4,6,8,10,12,14,16,18,20,22,24,26,28,30},{1,3,5,7,9,11,13,15,17,19,..., dimensions={0} | all-to-all | bytes 2097152 | tf_op jit(solution)/shard_map/all_to_all | solution.py:92
  148.9 0.1 reduce_sum.9
  148.9 0.6 broadcast_multiply_fusion
  (1 shorter events, 0.0 us)
Async XLA Ops:
  0.0 12.2 %copy-start.3 = (bf16[1024,64]{0,1:T(8,128)(2,1)S(1)}, bf16[1024,64]{0,1:T(8,128)(2,1)}, u32[]{:S(2)}) copy-start(bf16[1024,64]{0,1:T(8,128)(2,1)} %param.6) | copy-start | bytes 393220
  4.5 8.8 %collective-permute-start = (f16[64,1024]{1,0:T(8,128)(2,1)S(1)}, f16[64,1024]{1,0:T(8,128)(2,1)S(1)}, u32[]{:S(2)}, u32[]{:S(2)}) collective-permute-start(f16[64,1024]{1,0:T(8,128)(2,1)S(1)} %select_convert_fusion), channel_id=1, source_target_pairs={{0,512},{32,544},{64,576},{96,608},{128,640},{160,672},{192,704},{... | collective-permute-start | bytes 393224 | tf_op jit(solution)/shard_map/ppermute | solution.py:61
  86.5 1.9 %copy-start = (f16[16,128,1024]{2,1,0:T(8,128)(2,1)}, f16[16,128,1024]{2,1,0:T(8,128)(2,1)S(1)}, u32[]{:S(2)}) copy-start(f16[16,128,1024]{2,1,0:T(8,128)(2,1)S(1)} %all-gather.1) | copy-start | bytes 12582916
  100.3 2.2 %copy-start.1 = (bf16[2048,512]{1,0:T(8,128)(2,1)S(1)}, bf16[2048,512]{1,0:T(8,128)(2,1)}, u32[]{:S(2)}) copy-start(bf16[2048,512]{1,0:T(8,128)(2,1)} %get-tuple-element.18) | copy-start | bytes 6291460 | tf_op jit(solution)/shard_map/cond
  105.1 4.7 %collective-permute-start.1 = (f32[16,32,512]{2,1,0:T(8,128)S(1)}, f32[16,32,512]{2,1,0:T(8,128)}, u32[]{:S(2)}, u32[]{:S(2)}) collective-permute-start(f32[16,32,512]{2,1,0:T(8,128)S(1)} %dynamic-slice_bitcast_fusion), channel_id=1, source_target_pairs={{0,1},{1,0},{2,3},{3,2},{4,5},{5,4},{6,7},{7,6},{8,9},{9,8},{10,11... | collective-permute-start | bytes 3145736 | tf_op jit(solution)/shard_map/ppermute | solution.py:90

commit v2 on v0

v2 whole, which is shorter than its diff:
```python
import jax
import jax.numpy as jnp
from jax import lax
from jax.experimental import pallas as pl
from jax.experimental.pallas import tpu as pltpu
from jax.sharding import PartitionSpec as P

TILE = 64
Z = 16
CHIPS = 16
Y = 8
PEERS = 32
ROWS = 32
LANES = 128
BIAS = 253.0
STEP = 512
VMEM = 40 * 1024 * 1024
WHOLE = 62 * 1024 * 1024


def encode(amps, tiles):
    value = jnp.where(tiles > 0, amps.astype(jnp.float32), 0.0)
    size = jnp.maximum(jnp.abs(value), 2.0**-126)
    power = jnp.floor(jnp.log2(size))
    half = jnp.floor(power * 0.5)
    digits = jnp.round(size * jnp.exp2(-half) * jnp.exp2(half - power) * 128.0)
    high = digits >= 256.0
    low = digits < 128.0
    digits = jnp.where(high, digits * 0.5, jnp.where(low, digits * 2.0, digits))
    power = jnp.where(high, power + 1.0, jnp.where(low, power - 1.0, power))
    code = (power + (BIAS - 1.0)) * 128.0 + digits
    code = jnp.where(value < 0, -code, code)
    code = jnp.where(jnp.abs(value) < 2.0**-126, 0.0, code)
    return code.astype(jnp.int32).astype(jnp.int16)


def decode(codes):
    number = codes.astype(jnp.float32) * (1.0 / 128.0)
    whole = jnp.floor(jnp.abs(number))
    digits = number + jnp.where(number < 0, whole - 1.0, 1.0 - whole)
    return (digits * jnp.exp2(whole - BIAS)).astype(jnp.bfloat16)


def spread(tiles):
    shape = (tiles.shape[0], tiles.shape[0] * TILE)
    at = lax.broadcasted_iota(jnp.int32, shape, 1) // TILE == lax.broadcasted_iota(jnp.int32, shape, 0)
    return lax.dot_general(
        tiles.astype(jnp.float32), at.astype(jnp.float32), (((0,), (0,)), ((), ())), preferred_element_type=jnp.float32
    )


def keep(block, flags):
    rows = []
    for t in range(block.shape[0] // TILE):
        part = block[t * TILE : (t + 1) * TILE, :].astype(jnp.float32)
        rows.append(jnp.where(flags[t : t + 1, :] > 0, part, 0.0).astype(jnp.bfloat16))
    return jnp.concatenate(rows, axis=0)


def front_body(place, amps, tiles, ints, flags, codes, away, wide):
    step = pl.program_id(0)

    @pl.when(step == 0)
    def _():
        wide[...] = spread(flags[...])

    count = ints.shape[0] // TILE
    first = pl.multiple_of((1 - place[0] // 2) * Z + step * count, 8)
    away[...] = keep(ints[...], wide[pl.ds(first, count), :])
    codes[...] = encode(amps[...], tiles[...])


def product_body(place, codes, ints, flags, swapped, mine, theirs, kept, wide):
    x_lo = place[0] // 2
    core = place[0] % 2

    @pl.when(pl.program_id(0) == 0)
    def _():
        wide[...] = spread(flags[...])
        kept[...] = keep(ints[...], wide[pl.ds(pl.multiple_of(x_lo * Z, 8), Z), :])

    amps = decode(codes[...])

    def put(side, block):
        total = lax.dot_general(amps, block, (((0,), (0,)), ((), ())), preferred_element_type=jnp.float32)
        total = total.reshape(STEP // (2 * ROWS), 2, ROWS, total.shape[-1])
        mine[side] = jnp.where(core == 0, total[:, 0], total[:, 1])
        theirs[side] = jnp.where(core == 0, total[:, 1], total[:, 0])

    put(x_lo, kept[...])
    put(1 - x_lo, swapped[...])


def diagonal():
    shape = (ROWS, LANES)
    return lax.broadcasted_iota(jnp.int32, shape, 0) == lax.broadcasted_iota(jnp.int32, shape, 1)


def pack(totals, shares):
    lines = []
    at = 0
    for total in totals:
        top = jnp.max(jnp.abs(total), axis=1, keepdims=True)
        level = jnp.ceil(jnp.log2(jnp.maximum(top, 2.0**-110)) * 16.0)
        scaled = total * jnp.exp2(-level * (1.0 / 16.0)) * 32767.0
        whole = jnp.clip(jnp.round(scaled), -32767.0, 32767.0).astype(jnp.int32).astype(jnp.int16)
        for k in range(total.shape[1] // LANES):
            shares[at : at + ROWS, :] = whole[:, LANES * k : LANES * (k + 1)]
            at += ROWS
        lines.append(jnp.sum(jnp.where(diagonal(), level, 0.0), axis=0, keepdims=True))
    lines.append(jnp.zeros((16 - len(lines), LANES), jnp.float32))
    shares[at:, :] = jnp.concatenate(lines, axis=0).astype(jnp.int32).astype(jnp.int16)


def unpack(shares, i, parts):
    at = shares.shape[0] - 16
    line = shares[at:, :].astype(jnp.float32)[i : i + 1, :]
    level = jnp.sum(jnp.where(diagonal(), line, 0.0), axis=1, keepdims=True)
    scale = jnp.exp2(level * (1.0 / 16.0)) * (1.0 / 32767.0)
    at = i * parts * ROWS
    rows = [shares[at + ROWS * k : at + ROWS * (k + 1), :].astype(jnp.float32) * scale for k in range(parts)]
    return jnp.concatenate(rows, axis=1)


def pack_body(mine, theirs, shares):
    pack([mine[0, i] + theirs[0, i] for i in range(mine.shape[1])], shares.at[0])


def middle_body(came, shares):
    parts = (shares.shape[1] - 16) // ROWS
    for i in range(shares.shape[0]):
        total = sum(unpack(came.at[j], i, parts) for j in range(came.shape[0]))
        pack([total], shares.at[i])


def last_body(shares, out):
    out[...] = sum(unpack(shares.at[i], 0, out.shape[1] // LANES) for i in range(shares.shape[0]))


def per_device(amps, amp_tiles, ints, int_tiles):
    blk = lax.axis_index("blk")
    rep = lax.axis_index("rep")
    x_lo = lax.shift_right_logical(blk, 4)
    core = rep & 1
    place = (2 * x_lo + core).astype(jnp.int32).reshape(1)
    pairs = amps.shape[0]
    cols = ints.shape[1]
    half = ints.shape[0] // 2
    parts = cols // LANES
    tile_flags = int_tiles.T

    codes, away = pl.pallas_call(
        front_body,
        grid_spec=pltpu.PrefetchScalarGridSpec(
            num_scalar_prefetch=1,
            grid=(2,),
            in_specs=[
                pl.BlockSpec((TILE // 2, pairs), lambda s, place: (s, 0)),
                pl.BlockSpec((1, pairs), lambda s, place: (0, 0)),
                pl.BlockSpec((half // 2, cols), lambda s, place: (2 * (1 - place[0] // 2) + s, 0)),
                pl.BlockSpec(tile_flags.shape, lambda s, place: (0, 0)),
            ],
            out_specs=[
                pl.BlockSpec((TILE // 2, pairs), lambda s, place: (s, 0)),
                pl.BlockSpec((half // 2, cols), lambda s, place: (s, 0)),
            ],
            scratch_shapes=[pltpu.VMEM((2 * Z, cols), jnp.float32)],
        ),
        out_shape=[jax.ShapeDtypeStruct((TILE, pairs), jnp.int16), jax.ShapeDtypeStruct((half, cols), ints.dtype)],
        compiler_params=pltpu.CompilerParams(vmem_limit_bytes=WHOLE, dimension_semantics=("arbitrary",)),
        cost_estimate=pl.CostEstimate(flops=4_000_000, bytes_accessed=3 << 20, transcendentals=200_000),
    )(place, amps.T, amp_tiles.T, ints, tile_flags)

    swapped = lax.ppermute(away, "blk", [(b, b ^ Z) for b in range(2 * Z)])

    rings = [[h * Z + z for z in range(Z)] for h in range(2)]
    gathered = lax.all_gather(codes[None], "blk", axis=0, tiled=True, axis_index_groups=rings)
    gathered = gathered.reshape(half, pairs)

    group = STEP // (2 * ROWS)
    result = jax.ShapeDtypeStruct((2, CHIPS, ROWS, cols), jnp.float32)
    mine, theirs = pl.pallas_call(
        product_body,
        grid_spec=pltpu.PrefetchScalarGridSpec(
            num_scalar_prefetch=1,
            grid=(pairs // STEP,),
            in_specs=[
                pl.BlockSpec((half, STEP), lambda s, place: (0, s)),
                pl.BlockSpec((half, cols), lambda s, place: (place[0] // 2, 0)),
                pl.BlockSpec(tile_flags.shape, lambda s, place: (0, 0)),
                pl.BlockSpec((half, cols), lambda s, place: (0, 0)),
            ],
            out_specs=[pl.BlockSpec((2, group, ROWS, cols), lambda s, place: (0, s, 0, 0))] * 2,
            scratch_shapes=[pltpu.VMEM((half, cols), jnp.bfloat16), pltpu.VMEM((2 * Z, cols), jnp.float32)],
        ),
        out_shape=[result, result],
        compiler_params=pltpu.CompilerParams(vmem_limit_bytes=VMEM, dimension_semantics=("arbitrary",)),
        cost_estimate=pl.CostEstimate(flops=4 * pairs * half * cols, bytes_accessed=8 << 20, transcendentals=1 << 20),
    )(place, gathered, ints, tile_flags, swapped)

    theirs = lax.ppermute(theirs, "rep", [(r, r ^ 1) for r in range(2 * CHIPS)])

    peers = PEERS // Y
    block = Y * parts * ROWS + 16
    shares = pl.pallas_call(
        pack_body,
        grid=(peers,),
        in_specs=[pl.BlockSpec((1, Y, ROWS, cols), lambda s: (s // 2, s % 2, 0, 0))] * 2,
        out_specs=pl.BlockSpec((1, block, LANES), lambda s: (s, 0, 0)),
        out_shape=jax.ShapeDtypeStruct((peers, block, LANES), jnp.int16),
        compiler_params=pltpu.CompilerParams(vmem_limit_bytes=VMEM),
    )(mine, theirs)

    across = [
        [(h * Z + z) * 2 * CHIPS + g * CHIPS + 2 * y + c for h in range(2) for g in range(2)]
        for z in range(Z)
        for y in range(Y)
        for c in range(2)
    ]
    came = lax.all_to_all(shares, ("blk", "rep"), 0, 0, tiled=True, axis_index_groups=across)
    shares = pl.pallas_call(
        middle_body,
        out_shape=jax.ShapeDtypeStruct((Y, parts * ROWS + 16, LANES), jnp.int16),
        compiler_params=pltpu.CompilerParams(vmem_limit_bytes=VMEM),
    )(came)
    along = [[g * CHIPS + 2 * y + c for y in range(Y)] for g in range(2) for c in range(2)]
    shares = lax.all_to_all(shares, "rep", 0, 0, tiled=True, axis_index_groups=along)

    return pl.pallas_call(
        last_body,
        out_shape=jax.ShapeDtypeStruct((ROWS, cols), jnp.float32),
        compiler_params=pltpu.CompilerParams(vmem_limit_bytes=VMEM),
    )(shares)


def solution(mesh):
    return jax.shard_map(
        per_device,
        mesh=mesh,
        in_specs=(
            P(None, ("rep", "blk")),
            P(None, ("rep", "blk")),
            P("rep", "blk"),
            P("rep", "blk"),
        ),
        out_specs=P("rep", "blk"),
        check_vma=False,
    )
```

time: 310 us -> 113 us (0.36)
  the two profiles are of different devices: /device:TPU:16 before, /device:TPU:2 now
where the time goes in v2:
time: 113 us
  blocking collectives  81.5 us (72%)
  starting transfers between devices  17.1 us (15%)
  Pallas kernels  9.86 us (9%)
  waiting for transfers between devices  4.13 us (4%)
    all_gather x1, blocking collectives, per_device(): lax.all_gather(codes[None], 'blk', axis=0, tiled=True, axis_index_groups=...  43.5 us
    all_to_all x1, blocking collectives, per_device(): lax.all_to_all(shares, ('blk', 'rep'), 0, 0, tiled=True, axis_index_group...  19.4 us
    all_to_all x1, blocking collectives, per_device(): lax.all_to_all(shares, 'rep', 0, 0, tiled=True, axis_index_groups=along)  18.6 us
    ppermute x1, starting transfers between devices, per_device(): swapped = lax.ppermute(away, 'blk', [(b, b ^ Z) for b in range(2 * Z)])  15.2 us
    pallas_call x1, Pallas kernels, per_device(): pl.pallas_call(product_body, grid_spec=pltpu.PrefetchScalarGridSpec(num_s...  4.93 us
    ppermute x1, waiting for transfers between devices, per_device(): theirs = lax.ppermute(theirs, 'rep', [(r, r ^ 1) for r in range(2 * CHIPS)])  4.13 us
    pallas_call x1, Pallas kernels, per_device(): pl.pallas_call(front_body, grid_spec=pltpu.PrefetchScalarGridSpec(num_sca...  2.57 us
  transfers between devices with their start and end apart: 2, of which 1 were waited for; matrix products, arithmetic and copies ran while one was open for 0% of the time, Pallas kernels for 0%

profile of v2, /device:TPU:2, one launch (start us, length us, event | category | flops | bytes accessed | tf_op | source)
XLA Modules:
  0.0 112.7 jit_solution(15901706485546148227)
XLA Ops:
  0.0 0.0 copy-start.1
  0.0 2.6 %shard_map.46 = (s16[64,1024]{1,0:T(8,128)(2,1)}, bf16[1024,512]{1,0:T(8,128)(2,1)}) custom-call(s32[1]{0:T(128)} %bitcast.place, bf16[64,1024]{1,0:T(8,128)(2,1)} %bitcast.6, s32[1,1024]{1,0:T(1,128)} %bitcast.7, bf16[2048,512]{1,0:T(8,128)(2,1)} %ints.3, s32[8,32]{1,0:T(8,128)} %bitcast.4), custom_call_target="tpu_custom_call" | custom-call | flops 4000000 | bytes 3145728 | tf_op jit(solution)/shard_map/pallas_call | solution.py:152
  2.6 0.0 copy-start
  2.6 15.2 %collective-permute-start = (bf16[1024,512]{1,0:T(8,128)(2,1)}, bf16[1024,512]{1,0:T(8,128)(2,1)S(1)}, u32[]{:S(2)}, u32[]{:S(2)}) collective-permute-start(bf16[1024,512]{1,0:T(8,128)(2,1)} %get-tuple-element.10), channel_id=1, source_target_pairs={{0,512},{32,544},{64,576},{96,608},{128,640},{160,672},{192,704},{... | collective-permute-start | bytes 3145736 | tf_op jit(solution)/shard_map/ppermute | solution.py:174
  17.8 43.5 %all-gather.2.codes = s16[1024,1024]{1,0:T(8,128)(2,1)S(1)} all-gather(s16[64,1024]{1,0:T(8,128)(2,1)} %get-tuple-element.9), channel_id=2, replica_groups={{0,32,64,96,128,160,192,224,256,288,320,352,384,416,448,480},{512,544,5..., dimensions={0}, use_global_device_ids=true | all-gather | bytes 2228224 | tf_op jit(solution)/shard_map/all_gather | solution.py:177
  61.3 0.0 collective-permute-done.swapped
  61.3 0.0 copy-done.1
  61.3 0.0 copy-done
  61.4 4.9 %shard_map.47 = (f32[2,16,32,512]{3,2,1,0:T(8,128)S(1)}, f32[2,16,32,512]{3,2,1,0:T(8,128)S(1)}) custom-call(s32[1]{0:T(128)} %bitcast.place, s16[1024,1024]{1,0:T(8,128)(2,1)S(1)} %all-gather.2.codes, bf16[2048,512]{1,0:T(8,128)(2,1)S(1)} %copy-done, s32[8,32]{1,0:T(8,128)S(1)} %bitcast.5, bf16[1024,512]{1,0:T(8,128)(2,1)S(1)} %collective-permute-done.swapped), custom_call_target="tpu_custom_call" | custom-call | flops 2147483648 | bytes 8388608 | tf_op jit(solution)/shard_map/pallas_call | solution.py:182
  66.3 1.9 %collective-permute-start.1 = (f32[2,16,32,512]{3,2,1,0:T(8,128)S(1)}, f32[2,16,32,512]{3,2,1,0:T(8,128)S(1)}, u32[]{:S(2)}, u32[]{:S(2)}) collective-permute-start(f32[2,16,32,512]{3,2,1,0:T(8,128)S(1)} %get-tuple-element.12), channel_id=1, source_target_pairs={{0,1},{1,0},{2,3},{3,2},{4,5},{5,4},{6,7},{7,6},{8,9},{9,8},{10,11... | collective-permute-start | bytes 6291464 | tf_op jit(solution)/shard_map/ppermute | solution.py:201
  68.2 4.1 %collective-permute-done.1.theirs = f32[2,16,32,512]{3,2,1,0:T(8,128)S(1)} collective-permute-done((f32[2,16,32,512]{3,2,1,0:T(8,128)S(1)}, f32[2,16,32,512]{3,2,1,0:T(8,128)S(1)}, u32[]{:S(2)}, u32[]{:S(2)}) %collective-permute-start.1) | collective-permute-done | bytes 2097184 | tf_op jit(solution)/shard_map/ppermute | solution.py:201
  72.3 1.0 shard_map.48
  73.4 19.4 %all_to_all.10.came = s16[4,1040,128]{2,1,0:T(8,128)(2,1)S(1)} all-to-all(s16[4,1040,128]{2,1,0:T(8,128)(2,1)S(1)} %shard_map.48), channel_id=1, replica_groups={{0,16,512,528},{1,17,513,529},{2,18,514,530},{3,19,515,531},{4,20,516,5..., dimensions={0} | all-to-all | bytes 2129920 | tf_op jit(solution)/shard_map/all_to_all | solution.py:220
  92.7 0.6 shard_map.49
  93.3 18.6 %all_to_all.11.shares = s16[8,144,128]{2,1,0:T(8,128)(2,1)S(1)} all-to-all(s16[8,144,128]{2,1,0:T(8,128)(2,1)S(1)} %shard_map.49), channel_id=1, replica_groups={{0,2,4,6,8,10,12,14},{1,3,5,7,9,11,13,15},{16,18,20,22,24,26,28,30},{17..., dimensions={0} | all-to-all | bytes 589824 | tf_op jit(solution)/shard_map/all_to_all | solution.py:227
  111.9 0.8 shard_map.50
Async XLA Ops:
  0.0 61.3 %copy-start.1 = (s32[32,8]{0,1:T(8,128)S(1)}, s32[32,8]{0,1:T(8,128)}, u32[]{:S(2)}) copy-start(s32[32,8]{0,1:T(8,128)} %param.7) | copy-start | bytes 3076
  2.6 58.8 %copy-start = (bf16[2048,512]{1,0:T(8,128)(2,1)S(1)}, bf16[2048,512]{1,0:T(8,128)(2,1)}, u32[]{:S(2)}) copy-start(bf16[2048,512]{1,0:T(8,128)(2,1)} %ints.3) | copy-start | bytes 6291460
  2.6 58.8 %collective-permute-start = (bf16[1024,512]{1,0:T(8,128)(2,1)}, bf16[1024,512]{1,0:T(8,128)(2,1)S(1)}, u32[]{:S(2)}, u32[]{:S(2)}) collective-permute-start(bf16[1024,512]{1,0:T(8,128)(2,1)} %get-tuple-element.10), channel_id=1, source_target_pairs={{0,512},{32,544},{64,576},{96,608},{128,640},{160,672},{192,704},{... | collective-permute-start | bytes 3145736 | tf_op jit(solution)/shard_map/ppermute | solution.py:174
  66.3 6.1 %collective-permute-start.1 = (f32[2,16,32,512]{3,2,1,0:T(8,128)S(1)}, f32[2,16,32,512]{3,2,1,0:T(8,128)S(1)}, u32[]{:S(2)}, u32[]{:S(2)}) collective-permute-start(f32[2,16,32,512]{3,2,1,0:T(8,128)S(1)} %get-tuple-element.12), channel_id=1, source_target_pairs={{0,1},{1,0},{2,3},{3,2},{4,5},{5,4},{6,7},{7,6},{8,9},{9,8},{10,11... | collective-permute-start | bytes 6291464 | tf_op jit(solution)/shard_map/ppermute | solution.py:201

commit v3 on v2

--- a/solution.py
+++ b/solution.py
@@ -9,11 +9,10 @@
 Z = 16
 CHIPS = 16
 Y = 8
-PEERS = 32
 ROWS = 32
 LANES = 128
 BIAS = 253.0
-STEP = 512
+STEP = 256
 VMEM = 40 * 1024 * 1024
 WHOLE = 62 * 1024 * 1024
 
@@ -65,30 +64,26 @@
         wide[...] = spread(flags[...])
 
     count = ints.shape[0] // TILE
-    first = pl.multiple_of((1 - place[0] // 2) * Z + step * count, 8)
+    first = pl.multiple_of((1 - place[0] // 2 % 2) * Z + step * count, 8)
     away[...] = keep(ints[...], wide[pl.ds(first, count), :])
     codes[...] = encode(amps[...], tiles[...])
 
 
-def product_body(place, codes, ints, flags, swapped, mine, theirs, kept, wide):
-    x_lo = place[0] // 2
+def product_body(place, codes, ints, flags, swapped, mine, mine_far, theirs, theirs_far, kept, wide):
+    x_lo = place[0] // 2 % 2
     core = place[0] % 2
-
-    @pl.when(pl.program_id(0) == 0)
-    def _():
-        wide[...] = spread(flags[...])
-        kept[...] = keep(ints[...], wide[pl.ds(pl.multiple_of(x_lo * Z, 8), Z), :])
-
-    amps = decode(codes[...])
-
-    def put(side, block):
-        total = lax.dot_general(amps, block, (((0,), (0,)), ((), ())), preferred_element_type=jnp.float32)
-        total = total.reshape(STEP // (2 * ROWS), 2, ROWS, total.shape[-1])
-        mine[side] = jnp.where(core == 0, total[:, 0], total[:, 1])
-        theirs[side] = jnp.where(core == 0, total[:, 1], total[:, 0])
-
-    put(x_lo, kept[...])
-    put(1 - x_lo, swapped[...])
+    half = kept.shape[0]
+    wide[...] = spread(flags[...])
+    own = ints[pl.ds(pl.multiple_of(x_lo * half, half), half), :]
+    kept[...] = keep(own, wide[pl.ds(pl.multiple_of(x_lo * Z, Z), Z), :])
+    count = STEP // (2 * ROWS)
+    for s in range(codes.shape[1] // STEP):
+        amps = decode(codes[:, s * STEP : (s + 1) * STEP])
+        for block, ours, others in ((kept, mine, theirs), (swapped, mine_far, theirs_far)):
+            total = lax.dot_general(amps, block[...], (((0,), (0,)), ((), ())), preferred_element_type=jnp.float32)
+            total = total.reshape(count, 2, ROWS, total.shape[-1])
+            ours[s * count : (s + 1) * count] = jnp.where(core == 0, total[:, 0], total[:, 1])
+            others[s * count : (s + 1) * count] = jnp.where(core == 0, total[:, 1], total[:, 0])
 
 
 def diagonal():
@@ -122,14 +117,24 @@
     return jnp.concatenate(rows, axis=1)
 
 
-def pack_body(mine, theirs, shares):
-    pack([mine[0, i] + theirs[0, i] for i in range(mine.shape[1])], shares.at[0])
-
-
-def middle_body(came, shares):
+def near_body(place, mine, theirs, near):
+    half = 1 - place[0] // 4
+    pack([mine[half, i] + theirs[half, i] for i in range(Y)], near)
+
+
+def far_body(place, mine, theirs, near, low, far):
+    x_hi = place[0] // 4
+    for half, shares in ((x_hi, low), (1 - x_hi, far)):
+        pack([mine[half, i] + theirs[half, i] for i in range(Y)], shares)
+
+
+def middle_body(place, mine, theirs, near, low, far, shares):
     parts = (shares.shape[1] - 16) // ROWS
+    half = place[0] // 4
     for i in range(shares.shape[0]):
-        total = sum(unpack(came.at[j], i, parts) for j in range(came.shape[0]))
+        total = mine[half, i] + theirs[half, i]
+        for came in (near, low, far):
+            total += unpack(came, i, parts)
         pack([total], shares.at[i])
 
 
@@ -142,7 +147,7 @@
     rep = lax.axis_index("rep")
     x_lo = lax.shift_right_logical(blk, 4)
     core = rep & 1
-    place = (2 * x_lo + core).astype(jnp.int32).reshape(1)
+    place = (4 * lax.shift_right_logical(rep, 4) + 2 * x_lo + core).astype(jnp.int32).reshape(1)
     pairs = amps.shape[0]
     cols = ints.shape[1]
     half = ints.shape[0] // 2
@@ -157,7 +162,7 @@
             in_specs=[
                 pl.BlockSpec((TILE // 2, pairs), lambda s, place: (s, 0)),
                 pl.BlockSpec((1, pairs), lambda s, place: (0, 0)),
-                pl.BlockSpec((half // 2, cols), lambda s, place: (2 * (1 - place[0] // 2) + s, 0)),
+                pl.BlockSpec((half // 2, cols), lambda s, place: (2 * (1 - place[0] // 2 % 2) + s, 0)),
                 pl.BlockSpec(tile_flags.shape, lambda s, place: (0, 0)),
             ],
             out_specs=[
@@ -177,52 +182,56 @@
     gathered = lax.all_gather(codes[None], "blk", axis=0, tiled=True, axis_index_groups=rings)
     gathered = gathered.reshape(half, pairs)
 
-    group = STEP // (2 * ROWS)
-    result = jax.ShapeDtypeStruct((2, CHIPS, ROWS, cols), jnp.float32)
-    mine, theirs = pl.pallas_call(
+    inside = pl.BlockSpec(memory_space=pltpu.VMEM)
+    scalar = pl.BlockSpec(memory_space=pltpu.SMEM)
+    result = jax.ShapeDtypeStruct((CHIPS, ROWS, cols), jnp.float32)
+    mine, mine_far, theirs, theirs_far = pl.pallas_call(
         product_body,
-        grid_spec=pltpu.PrefetchScalarGridSpec(
-            num_scalar_prefetch=1,
-            grid=(pairs // STEP,),
-            in_specs=[
-                pl.BlockSpec((half, STEP), lambda s, place: (0, s)),
-                pl.BlockSpec((half, cols), lambda s, place: (place[0] // 2, 0)),
-                pl.BlockSpec(tile_flags.shape, lambda s, place: (0, 0)),
-                pl.BlockSpec((half, cols), lambda s, place: (0, 0)),
-            ],
-            out_specs=[pl.BlockSpec((2, group, ROWS, cols), lambda s, place: (0, s, 0, 0))] * 2,
-            scratch_shapes=[pltpu.VMEM((half, cols), jnp.bfloat16), pltpu.VMEM((2 * Z, cols), jnp.float32)],
-        ),
-        out_shape=[result, result],
-        compiler_params=pltpu.CompilerParams(vmem_limit_bytes=VMEM, dimension_semantics=("arbitrary",)),
+        in_specs=[scalar] + [inside] * 4,
+        out_specs=[inside] * 4,
+        scratch_shapes=[pltpu.VMEM((half, cols), jnp.bfloat16), pltpu.VMEM((2 * Z, cols), jnp.float32)],
+        out_shape=[result] * 4,
+        compiler_params=pltpu.CompilerParams(vmem_limit_bytes=VMEM),
         cost_estimate=pl.CostEstimate(flops=4 * pairs * half * cols, bytes_accessed=8 << 20, transcendentals=1 << 20),
     )(place, gathered, ints, tile_flags, swapped)
 
-    theirs = lax.ppermute(theirs, "rep", [(r, r ^ 1) for r in range(2 * CHIPS)])
-
-    peers = PEERS // Y
+    n = 2 * CHIPS
+    swap = [(r, r ^ 1) for r in range(n)]
+    theirs = lax.ppermute(theirs, "rep", swap).reshape(2, Y, ROWS, cols)
+    theirs_far = lax.ppermute(theirs_far, "rep", swap).reshape(2, Y, ROWS, cols)
+    mine = mine.reshape(2, Y, ROWS, cols)
+    mine_far = mine_far.reshape(2, Y, ROWS, cols)
+
     block = Y * parts * ROWS + 16
-    shares = pl.pallas_call(
-        pack_body,
-        grid=(peers,),
-        in_specs=[pl.BlockSpec((1, Y, ROWS, cols), lambda s: (s // 2, s % 2, 0, 0))] * 2,
-        out_specs=pl.BlockSpec((1, block, LANES), lambda s: (s, 0, 0)),
-        out_shape=jax.ShapeDtypeStruct((peers, block, LANES), jnp.int16),
-        compiler_params=pltpu.CompilerParams(vmem_limit_bytes=VMEM),
-    )(mine, theirs)
-
-    across = [
-        [(h * Z + z) * 2 * CHIPS + g * CHIPS + 2 * y + c for h in range(2) for g in range(2)]
-        for z in range(Z)
-        for y in range(Y)
-        for c in range(2)
-    ]
-    came = lax.all_to_all(shares, ("blk", "rep"), 0, 0, tiled=True, axis_index_groups=across)
+    sent = jax.ShapeDtypeStruct((block, LANES), jnp.int16)
+    near = pl.pallas_call(
+        near_body,
+        in_specs=[scalar, inside, inside],
+        out_specs=inside,
+        out_shape=sent,
+        compiler_params=pltpu.CompilerParams(vmem_limit_bytes=VMEM),
+        cost_estimate=pl.CostEstimate(flops=4 << 20, bytes_accessed=2 << 20, transcendentals=0),
+    )(place, mine, theirs)
+    low, far = pl.pallas_call(
+        far_body,
+        in_specs=[scalar, inside, inside, pl.BlockSpec(memory_space=pl.ANY)],
+        out_specs=[inside, inside],
+        out_shape=[sent, sent],
+        compiler_params=pltpu.CompilerParams(vmem_limit_bytes=VMEM),
+        cost_estimate=pl.CostEstimate(flops=8 << 20, bytes_accessed=4 << 20, transcendentals=0),
+    )(place, mine_far, theirs_far, near)
+    near = lax.ppermute(near, "rep", [(r, r ^ CHIPS) for r in range(n)])
+    low = lax.ppermute(low, "blk", [(b, b ^ Z) for b in range(2 * Z)])
+    far = lax.ppermute(
+        far, ("blk", "rep"), [(b * n + r, (b ^ Z) * n + (r ^ CHIPS)) for b in range(2 * Z) for r in range(n)]
+    )
     shares = pl.pallas_call(
         middle_body,
+        in_specs=[scalar] + [inside] * 5,
+        out_specs=inside,
         out_shape=jax.ShapeDtypeStruct((Y, parts * ROWS + 16, LANES), jnp.int16),
         compiler_params=pltpu.CompilerParams(vmem_limit_bytes=VMEM),
-    )(came)
+    )(place, mine, theirs, near, low, far)
     along = [[g * CHIPS + 2 * y + c for y in range(Y)] for g in range(2) for c in range(2)]
     shares = lax.all_to_all(shares, "rep", 0, 0, tiled=True, axis_index_groups=along)
 

time: 113 us -> 109 us (0.965)
  the two profiles are of different devices: /device:TPU:2 before, /device:TPU:4 now
where the time goes in v3:
time: 109 us
  blocking collectives  75.6 us (69%)
  starting transfers between devices  17.4 us (16%)
  Pallas kernels  8.29 us (8%)
  waiting for transfers between devices  7.48 us (7%)
    all_gather x1, blocking collectives, per_device(): lax.all_gather(codes[None], 'blk', axis=0, tiled=True, axis_index_groups=...  56.2 us
    all_to_all x1, blocking collectives, per_device(): lax.all_to_all(shares, 'rep', 0, 0, tiled=True, axis_index_groups=along)  19.4 us
    ppermute x1, starting transfers between devices, per_device(): lax.ppermute(far, ('blk', 'rep'), [(b * n + r, (b ^ Z) * n + (r ^ CHIPS))...  4.06 us
    pallas_call x1, Pallas kernels, per_device(): pl.pallas_call(product_body, in_specs=[scalar] + [inside] * 4, out_specs=...  3.8 us
    ppermute x1, waiting for transfers between devices, per_device(): low = lax.ppermute(low, 'blk', [(b, b ^ Z) for b in range(2 * Z)])  3.31 us
    ppermute x1, starting transfers between devices, per_device(): swapped = lax.ppermute(away, 'blk', [(b, b ^ Z) for b in range(2 * Z)])  3.23 us
    ppermute x1, starting transfers between devices, per_device(): low = lax.ppermute(low, 'blk', [(b, b ^ Z) for b in range(2 * Z)])  3.04 us
    ppermute x1, starting transfers between devices, per_device(): near = lax.ppermute(near, 'rep', [(r, r ^ CHIPS) for r in range(n)])  2.71 us
  transfers between devices with their start and end apart: 6, of which 4 were waited for; matrix products, arithmetic and copies ran while one was open for 0% of the time, Pallas kernels for 1%

profile of v3, /device:TPU:4, one launch (start us, length us, event | category | flops | bytes accessed | tf_op | source)
XLA Modules:
  0.0 108.8 jit_solution(649721538320274542)
XLA Ops:
  0.0 0.0 copy-start.1
  0.0 2.5 %shard_map.46 = (s16[64,1024]{1,0:T(8,128)(2,1)}, bf16[1024,512]{1,0:T(8,128)(2,1)}) custom-call(s32[1]{0:T(128)} %bitcast.place, bf16[64,1024]{1,0:T(8,128)(2,1)} %bitcast.16, s32[1,1024]{1,0:T(1,128)} %bitcast.17, bf16[2048,512]{1,0:T(8,128)(2,1)} %ints.3, s32[8,32]{1,0:T(8,128)} %bitcast.14), custom_call_target="tpu_custom_call" | custom-call | flops 4000000 | bytes 3145728 | tf_op jit(solution)/shard_map/pallas_call | solution.py:157
  2.5 0.0 copy-start
  2.6 3.2 %collective-permute-start = (bf16[1024,512]{1,0:T(8,128)(2,1)}, bf16[1024,512]{1,0:T(8,128)(2,1)S(1)}, u32[]{:S(2)}, u32[]{:S(2)}) collective-permute-start(bf16[1024,512]{1,0:T(8,128)(2,1)} %get-tuple-element.14), channel_id=1, source_target_pairs={{0,512},{32,544},{64,576},{96,608},{128,640},{160,672},{192,704},{... | collective-permute-start | bytes 3145736 | tf_op jit(solution)/shard_map/ppermute | solution.py:179
  5.8 56.2 %all-gather.2.codes = s16[1024,1024]{1,0:T(8,128)(2,1)S(1)} all-gather(s16[64,1024]{1,0:T(8,128)(2,1)} %get-tuple-element.13), channel_id=2, replica_groups={{0,32,64,96,128,160,192,224,256,288,320,352,384,416,448,480},{512,544,5..., dimensions={0}, use_global_device_ids=true | all-gather | bytes 2228224 | tf_op jit(solution)/shard_map/all_gather | solution.py:182
  62.0 0.0 collective-permute-done.swapped
  62.0 0.0 copy-done.1
  62.0 0.0 copy-done
  62.0 3.8 %shard_map.47 = (f32[16,32,512]{2,1,0:T(8,128)S(1)}, f32[16,32,512]{2,1,0:T(8,128)S(1)}, f32[16,32,512]{2,1,0:T(8,128)S(1)}, f32[16,32,512]{2,1,0:T(8,128)S(1)}) custom-call(s32[1]{0:T(128)} %bitcast.place, s16[1024,1024]{1,0:T(8,128)(2,1)S(1)} %all-gather.2.codes, bf16[2048,512]{1,0:T(8,128)(2,1)S(1)} %copy-done, s32[8,32]{1,0:T(8,128)S(1)} %bitcast.15, ...), custom_call_target="tpu_custom_call" | custom-call | flops 2147483648 | bytes 8388608 | tf_op jit(solution)/shard_map/pallas_call | solution.py:188
  65.8 1.9 %collective-permute-start.1 = (f32[16,32,512]{2,1,0:T(8,128)S(1)}, f32[16,32,512]{2,1,0:T(8,128)S(1)}, u32[]{:S(2)}, u32[]{:S(2)}) collective-permute-start(f32[16,32,512]{2,1,0:T(8,128)S(1)} %get-tuple-element.16), channel_id=1, source_target_pairs={{0,1},{1,0},{2,3},{3,2},{4,5},{5,4},{6,7},{7,6},{8,9},{9,8},{10,11... | collective-permute-start | bytes 3145736 | tf_op jit(solution)/shard_map/ppermute | solution.py:200
  67.7 2.4 %collective-permute-start.3 = (f32[16,32,512]{2,1,0:T(8,128)S(1)}, f32[16,32,512]{2,1,0:T(8,128)S(1)}, u32[]{:S(2)}, u32[]{:S(2)}) collective-permute-start(f32[16,32,512]{2,1,0:T(8,128)S(1)} %get-tuple-element.18), channel_id=1, source_target_pairs={{0,1},{1,0},{2,3},{3,2},{4,5},{5,4},{6,7},{7,6},{8,9},{9,8},{10,11... | collective-permute-start | bytes 3145736 | tf_op jit(solution)/shard_map/ppermute | solution.py:201
  70.1 0.2 collective-permute-done.1
  70.4 0.2 shard_map.48.near
  70.6 2.7 %collective-permute-start.2 = (s16[1040,128]{1,0:T(8,128)(2,1)S(1)}, s16[1040,128]{1,0:T(8,128)(2,1)S(1)}, u32[]{:S(2)}, u32[]{:S(2)}) collective-permute-start(s16[1040,128]{1,0:T(8,128)(2,1)S(1)} %shard_map.48.near), channel_id=1, source_target_pairs={{0,16},{1,17},{2,18},{3,19},{4,20},{5,21},{6,22},{7,23},{8,24},{9,... | collective-permute-start | bytes 798728 | tf_op jit(solution)/shard_map/ppermute | solution.py:223
  73.3 0.0 collective-permute-done.3
  73.3 0.4 shard_map.49
  73.8 3.0 %collective-permute-start.4 = (s16[1040,128]{1,0:T(8,128)(2,1)S(1)}, s16[1040,128]{1,0:T(8,128)(2,1)S(1)}, u32[]{:S(2)}, u32[]{:S(2)}) collective-permute-start(s16[1040,128]{1,0:T(8,128)(2,1)S(1)} %get-tuple-element.19), channel_id=1, source_target_pairs={{0,512},{32,544},{64,576},{96,608},{128,640},{160,672},{192,704},{... | collective-permute-start | bytes 798728 | tf_op jit(solution)/shard_map/ppermute | solution.py:224
  76.8 4.1 %collective-permute-start.5 = (s16[1040,128]{1,0:T(8,128)(2,1)S(1)}, s16[1040,128]{1,0:T(8,128)(2,1)S(1)}, u32[]{:S(2)}, u32[]{:S(2)}) collective-permute-start(s16[1040,128]{1,0:T(8,128)(2,1)S(1)} %get-tuple-element.20), channel_id=1, source_target_pairs={{0,528},{1,529},{2,530},{3,531},{4,532},{5,533},{6,534},{7,535},{8... | collective-permute-start | bytes 798728 | tf_op jit(solution)/shard_map/ppermute | solution.py:225
  80.9 2.4 %collective-permute-done.2.near = s16[1040,128]{1,0:T(8,128)(2,1)S(1)} collective-permute-done((s16[1040,128]{1,0:T(8,128)(2,1)S(1)}, s16[1040,128]{1,0:T(8,128)(2,1)S(1)}, u32[]{:S(2)}, u32[]{:S(2)}) %collective-permute-start.2) | collective-permute-done | bytes 266272 | tf_op jit(solution)/shard_map/ppermute | solution.py:223
  83.2 3.3 %collective-permute-done.4.low = s16[1040,128]{1,0:T(8,128)(2,1)S(1)} collective-permute-done((s16[1040,128]{1,0:T(8,128)(2,1)S(1)}, s16[1040,128]{1,0:T(8,128)(2,1)S(1)}, u32[]{:S(2)}, u32[]{:S(2)}) %collective-permute-start.4) | collective-permute-done | bytes 266272 | tf_op jit(solution)/shard_map/ppermute | solution.py:224
  86.5 1.6 %collective-permute-done.5.far = s16[1040,128]{1,0:T(8,128)(2,1)S(1)} collective-permute-done((s16[1040,128]{1,0:T(8,128)(2,1)S(1)}, s16[1040,128]{1,0:T(8,128)(2,1)S(1)}, u32[]{:S(2)}, u32[]{:S(2)}) %collective-permute-start.5) | collective-permute-done | bytes 266272 | tf_op jit(solution)/shard_map/ppermute | solution.py:225
  88.1 0.5 shard_map.50
  88.7 19.4 %all_to_all.5.shares = s16[8,144,128]{2,1,0:T(8,128)(2,1)S(1)} all-to-all(s16[8,144,128]{2,1,0:T(8,128)(2,1)S(1)} %shard_map.50), channel_id=1, replica_groups={{0,2,4,6,8,10,12,14},{1,3,5,7,9,11,13,15},{16,18,20,22,24,26,28,30},{17..., dimensions={0} | all-to-all | bytes 589824 | tf_op jit(solution)/shard_map/all_to_all | solution.py:236
  108.0 0.8 shard_map.51
Async XLA Ops:
  0.0 62.0 %copy-start.1 = (s32[32,8]{0,1:T(8,128)S(1)}, s32[32,8]{0,1:T(8,128)}, u32[]{:S(2)}) copy-start(s32[32,8]{0,1:T(8,128)} %param.7) | copy-start | bytes 3076
  2.5 59.4 %copy-start = (bf16[2048,512]{1,0:T(8,128)(2,1)S(1)}, bf16[2048,512]{1,0:T(8,128)(2,1)}, u32[]{:S(2)}) copy-start(bf16[2048,512]{1,0:T(8,128)(2,1)} %ints.3) | copy-start | bytes 6291460
  2.6 59.4 %collective-permute-start = (bf16[1024,512]{1,0:T(8,128)(2,1)}, bf16[1024,512]{1,0:T(8,128)(2,1)S(1)}, u32[]{:S(2)}, u32[]{:S(2)}) collective-permute-start(bf16[1024,512]{1,0:T(8,128)(2,1)} %get-tuple-element.14), channel_id=1, source_target_pairs={{0,512},{32,544},{64,576},{96,608},{128,640},{160,672},{192,704},{... | collective-permute-start | bytes 3145736 | tf_op jit(solution)/shard_map/ppermute | solution.py:179
  65.8 4.6 %collective-permute-start.1 = (f32[16,32,512]{2,1,0:T(8,128)S(1)}, f32[16,32,512]{2,1,0:T(8,128)S(1)}, u32[]{:S(2)}, u32[]{:S(2)}) collective-permute-start(f32[16,32,512]{2,1,0:T(8,128)S(1)} %get-tuple-element.16), channel_id=1, source_target_pairs={{0,1},{1,0},{2,3},{3,2},{4,5},{5,4},{6,7},{7,6},{8,9},{9,8},{10,11... | collective-permute-start | bytes 3145736 | tf_op jit(solution)/shard_map/ppermute | solution.py:200
  67.7 5.6 %collective-permute-start.3 = (f32[16,32,512]{2,1,0:T(8,128)S(1)}, f32[16,32,512]{2,1,0:T(8,128)S(1)}, u32[]{:S(2)}, u32[]{:S(2)}) collective-permute-start(f32[16,32,512]{2,1,0:T(8,128)S(1)} %get-tuple-element.18), channel_id=1, source_target_pairs={{0,1},{1,0},{2,3},{3,2},{4,5},{5,4},{6,7},{7,6},{8,9},{9,8},{10,11... | collective-permute-start | bytes 3145736 | tf_op jit(solution)/shard_map/ppermute | solution.py:201
  70.6 12.6 %collective-permute-start.2 = (s16[1040,128]{1,0:T(8,128)(2,1)S(1)}, s16[1040,128]{1,0:T(8,128)(2,1)S(1)}, u32[]{:S(2)}, u32[]{:S(2)}) collective-permute-start(s16[1040,128]{1,0:T(8,128)(2,1)S(1)} %shard_map.48.near), channel_id=1, source_target_pairs={{0,16},{1,17},{2,18},{3,19},{4,20},{5,21},{6,22},{7,23},{8,24},{9,... | collective-permute-start | bytes 798728 | tf_op jit(solution)/shard_map/ppermute | solution.py:223
  73.8 12.8 %collective-permute-start.4 = (s16[1040,128]{1,0:T(8,128)(2,1)S(1)}, s16[1040,128]{1,0:T(8,128)(2,1)S(1)}, u32[]{:S(2)}, u32[]{:S(2)}) collective-permute-start(s16[1040,128]{1,0:T(8,128)(2,1)S(1)} %get-tuple-element.19), channel_id=1, source_target_pairs={{0,512},{32,544},{64,576},{96,608},{128,640},{160,672},{192,704},{... | collective-permute-start | bytes 798728 | tf_op jit(solution)/shard_map/ppermute | solution.py:224
  76.8 11.3 %collective-permute-start.5 = (s16[1040,128]{1,0:T(8,128)(2,1)S(1)}, s16[1040,128]{1,0:T(8,128)(2,1)S(1)}, u32[]{:S(2)}, u32[]{:S(2)}) collective-permute-start(s16[1040,128]{1,0:T(8,128)(2,1)S(1)} %get-tuple-element.20), channel_id=1, source_target_pairs={{0,528},{1,529},{2,530},{3,531},{4,532},{5,533},{6,534},{7,535},{8... | collective-permute-start | bytes 798728 | tf_op jit(solution)/shard_map/ppermute | solution.py:225

commit v4 on v3

--- a/solution.py
+++ b/solution.py
@@ -53,7 +53,7 @@
     for t in range(block.shape[0] // TILE):
         part = block[t * TILE : (t + 1) * TILE, :].astype(jnp.float32)
         rows.append(jnp.where(flags[t : t + 1, :] > 0, part, 0.0).astype(jnp.bfloat16))
-    return jnp.concatenate(rows, axis=0)
+    return jnp.concatenate(rows[::-1], axis=0)
 
 
 def front_body(place, amps, tiles, ints, flags, codes, away, wide):
@@ -167,7 +167,7 @@
             ],
             out_specs=[
                 pl.BlockSpec((TILE // 2, pairs), lambda s, place: (s, 0)),
-                pl.BlockSpec((half // 2, cols), lambda s, place: (s, 0)),
+                pl.BlockSpec((half // 2, cols), lambda s, place: (1 - s, 0)),
             ],
             scratch_shapes=[pltpu.VMEM((2 * Z, cols), jnp.float32)],
         ),
@@ -178,7 +178,7 @@
 
     swapped = lax.ppermute(away, "blk", [(b, b ^ Z) for b in range(2 * Z)])
 
-    rings = [[h * Z + z for z in range(Z)] for h in range(2)]
+    rings = [[h * Z + z for z in reversed(range(Z))] for h in range(2)]
     gathered = lax.all_gather(codes[None], "blk", axis=0, tiled=True, axis_index_groups=rings)
     gathered = gathered.reshape(half, pairs)
 

time: 109 us -> 108 us (level)
  blocking collectives: 75.6 us -> 74.2 us
    all_gather x1, blocking collectives: 56.2 us -> 54.9 us  [per_device(): lax.all_gather(codes[None], 'blk', axis=0, tiled=True, axis_index_groups=...]
where the time goes in v4:
time: 108 us
  blocking collectives  74.2 us (69%)
  starting transfers between devices  17.4 us (16%)
  Pallas kernels  8.34 us (8%)
  waiting for transfers between devices  7.48 us (7%)
    all_gather x1, blocking collectives, per_device(): lax.all_gather(codes[None], 'blk', axis=0, tiled=True, axis_index_groups=...  54.9 us
    all_to_all x1, blocking collectives, per_device(): lax.all_to_all(shares, 'rep', 0, 0, tiled=True, axis_index_groups=along)  19.4 us
    ppermute x1, starting transfers between devices, per_device(): lax.ppermute(far, ('blk', 'rep'), [(b * n + r, (b ^ Z) * n + (r ^ CHIPS))...  4.06 us
    pallas_call x1, Pallas kernels, per_device(): pl.pallas_call(product_body, in_specs=[scalar] + [inside] * 4, out_specs=...  3.82 us
    ppermute x1, waiting for transfers between devices, per_device(): low = lax.ppermute(low, 'blk', [(b, b ^ Z) for b in range(2 * Z)])  3.31 us
    ppermute x1, starting transfers between devices, per_device(): swapped = lax.ppermute(away, 'blk', [(b, b ^ Z) for b in range(2 * Z)])  3.23 us
    ppermute x1, starting transfers between devices, per_device(): low = lax.ppermute(low, 'blk', [(b, b ^ Z) for b in range(2 * Z)])  3.05 us
    ppermute x1, starting transfers between devices, per_device(): near = lax.ppermute(near, 'rep', [(r, r ^ CHIPS) for r in range(n)])  2.71 us
  transfers between devices with their start and end apart: 6, of which 4 were waited for; matrix products, arithmetic and copies ran while one was open for 0% of the time, Pallas kernels for 1%

profile of v4, /device:TPU:4, one launch (start us, length us, event | category | flops | bytes accessed | tf_op | source)
XLA Modules:
  0.0 107.5 jit_solution(18130144085590195470)
XLA Ops:
  0.0 0.0 copy-start.1
  0.0 2.6 %shard_map.46 = (s16[64,1024]{1,0:T(8,128)(2,1)}, bf16[1024,512]{1,0:T(8,128)(2,1)}) custom-call(s32[1]{0:T(128)} %bitcast.place, bf16[64,1024]{1,0:T(8,128)(2,1)} %bitcast.16, s32[1,1024]{1,0:T(1,128)} %bitcast.17, bf16[2048,512]{1,0:T(8,128)(2,1)} %ints.3, s32[8,32]{1,0:T(8,128)} %bitcast.14), custom_call_target="tpu_custom_call" | custom-call | flops 4000000 | bytes 3145728 | tf_op jit(solution)/shard_map/pallas_call | solution.py:157
  2.6 0.0 copy-start
  2.6 3.2 %collective-permute-start = (bf16[1024,512]{1,0:T(8,128)(2,1)}, bf16[1024,512]{1,0:T(8,128)(2,1)S(1)}, u32[]{:S(2)}, u32[]{:S(2)}) collective-permute-start(bf16[1024,512]{1,0:T(8,128)(2,1)} %get-tuple-element.14), channel_id=1, source_target_pairs={{0,512},{32,544},{64,576},{96,608},{128,640},{160,672},{192,704},{... | collective-permute-start | bytes 3145736 | tf_op jit(solution)/shard_map/ppermute | solution.py:179
  5.8 54.9 %all-gather.2.codes = s16[1024,1024]{1,0:T(8,128)(2,1)S(1)} all-gather(s16[64,1024]{1,0:T(8,128)(2,1)} %get-tuple-element.13), channel_id=2, replica_groups={{480,448,416,384,352,320,288,256,224,192,160,128,96,64,32,0},{992,960,9..., dimensions={0}, use_global_device_ids=true | all-gather | bytes 2228224 | tf_op jit(solution)/shard_map/all_gather | solution.py:182
  60.7 0.0 collective-permute-done.swapped
  60.7 0.0 copy-done.1
  60.7 0.0 copy-done
  60.7 3.8 %shard_map.47 = (f32[16,32,512]{2,1,0:T(8,128)S(1)}, f32[16,32,512]{2,1,0:T(8,128)S(1)}, f32[16,32,512]{2,1,0:T(8,128)S(1)}, f32[16,32,512]{2,1,0:T(8,128)S(1)}) custom-call(s32[1]{0:T(128)} %bitcast.place, s16[1024,1024]{1,0:T(8,128)(2,1)S(1)} %all-gather.2.codes, bf16[2048,512]{1,0:T(8,128)(2,1)S(1)} %copy-done, s32[8,32]{1,0:T(8,128)S(1)} %bitcast.15, ...), custom_call_target="tpu_custom_call" | custom-call | flops 2147483648 | bytes 8388608 | tf_op jit(solution)/shard_map/pallas_call | solution.py:188
  64.5 1.9 %collective-permute-start.1 = (f32[16,32,512]{2,1,0:T(8,128)S(1)}, f32[16,32,512]{2,1,0:T(8,128)S(1)}, u32[]{:S(2)}, u32[]{:S(2)}) collective-permute-start(f32[16,32,512]{2,1,0:T(8,128)S(1)} %get-tuple-element.16), channel_id=1, source_target_pairs={{0,1},{1,0},{2,3},{3,2},{4,5},{5,4},{6,7},{7,6},{8,9},{9,8},{10,11... | collective-permute-start | bytes 3145736 | tf_op jit(solution)/shard_map/ppermute | solution.py:200
  66.4 2.4 %collective-permute-start.3 = (f32[16,32,512]{2,1,0:T(8,128)S(1)}, f32[16,32,512]{2,1,0:T(8,128)S(1)}, u32[]{:S(2)}, u32[]{:S(2)}) collective-permute-start(f32[16,32,512]{2,1,0:T(8,128)S(1)} %get-tuple-element.18), channel_id=1, source_target_pairs={{0,1},{1,0},{2,3},{3,2},{4,5},{5,4},{6,7},{7,6},{8,9},{9,8},{10,11... | collective-permute-start | bytes 3145736 | tf_op jit(solution)/shard_map/ppermute | solution.py:201
  68.9 0.2 collective-permute-done.1
  69.1 0.2 shard_map.48.near
  69.3 2.7 %collective-permute-start.2 = (s16[1040,128]{1,0:T(8,128)(2,1)S(1)}, s16[1040,128]{1,0:T(8,128)(2,1)S(1)}, u32[]{:S(2)}, u32[]{:S(2)}) collective-permute-start(s16[1040,128]{1,0:T(8,128)(2,1)S(1)} %shard_map.48.near), channel_id=1, source_target_pairs={{0,16},{1,17},{2,18},{3,19},{4,20},{5,21},{6,22},{7,23},{8,24},{9,... | collective-permute-start | bytes 798728 | tf_op jit(solution)/shard_map/ppermute | solution.py:223
  72.0 0.0 collective-permute-done.3
  72.0 0.4 shard_map.49
  72.5 3.1 %collective-permute-start.4 = (s16[1040,128]{1,0:T(8,128)(2,1)S(1)}, s16[1040,128]{1,0:T(8,128)(2,1)S(1)}, u32[]{:S(2)}, u32[]{:S(2)}) collective-permute-start(s16[1040,128]{1,0:T(8,128)(2,1)S(1)} %get-tuple-element.19), channel_id=1, source_target_pairs={{0,512},{32,544},{64,576},{96,608},{128,640},{160,672},{192,704},{... | collective-permute-start | bytes 798728 | tf_op jit(solution)/shard_map/ppermute | solution.py:224
  75.5 4.1 %collective-permute-start.5 = (s16[1040,128]{1,0:T(8,128)(2,1)S(1)}, s16[1040,128]{1,0:T(8,128)(2,1)S(1)}, u32[]{:S(2)}, u32[]{:S(2)}) collective-permute-start(s16[1040,128]{1,0:T(8,128)(2,1)S(1)} %get-tuple-element.20), channel_id=1, source_target_pairs={{0,528},{1,529},{2,530},{3,531},{4,532},{5,533},{6,534},{7,535},{8... | collective-permute-start | bytes 798728 | tf_op jit(solution)/shard_map/ppermute | solution.py:225
  79.6 2.4 %collective-permute-done.2.near = s16[1040,128]{1,0:T(8,128)(2,1)S(1)} collective-permute-done((s16[1040,128]{1,0:T(8,128)(2,1)S(1)}, s16[1040,128]{1,0:T(8,128)(2,1)S(1)}, u32[]{:S(2)}, u32[]{:S(2)}) %collective-permute-start.2) | collective-permute-done | bytes 266272 | tf_op jit(solution)/shard_map/ppermute | solution.py:223
  81.9 3.3 %collective-permute-done.4.low = s16[1040,128]{1,0:T(8,128)(2,1)S(1)} collective-permute-done((s16[1040,128]{1,0:T(8,128)(2,1)S(1)}, s16[1040,128]{1,0:T(8,128)(2,1)S(1)}, u32[]{:S(2)}, u32[]{:S(2)}) %collective-permute-start.4) | collective-permute-done | bytes 266272 | tf_op jit(solution)/shard_map/ppermute | solution.py:224
  85.3 1.6 %collective-permute-done.5.far = s16[1040,128]{1,0:T(8,128)(2,1)S(1)} collective-permute-done((s16[1040,128]{1,0:T(8,128)(2,1)S(1)}, s16[1040,128]{1,0:T(8,128)(2,1)S(1)}, u32[]{:S(2)}, u32[]{:S(2)}) %collective-permute-start.5) | collective-permute-done | bytes 266272 | tf_op jit(solution)/shard_map/ppermute | solution.py:225
  86.9 0.5 shard_map.50
  87.4 19.4 %all_to_all.5.shares = s16[8,144,128]{2,1,0:T(8,128)(2,1)S(1)} all-to-all(s16[8,144,128]{2,1,0:T(8,128)(2,1)S(1)} %shard_map.50), channel_id=1, replica_groups={{0,2,4,6,8,10,12,14},{1,3,5,7,9,11,13,15},{16,18,20,22,24,26,28,30},{17..., dimensions={0} | all-to-all | bytes 589824 | tf_op jit(solution)/shard_map/all_to_all | solution.py:236
  106.7 0.8 shard_map.51
Async XLA Ops:
  0.0 60.7 %copy-start.1 = (s32[32,8]{0,1:T(8,128)S(1)}, s32[32,8]{0,1:T(8,128)}, u32[]{:S(2)}) copy-start(s32[32,8]{0,1:T(8,128)} %param.7) | copy-start | bytes 3076
  2.6 58.1 %copy-start = (bf16[2048,512]{1,0:T(8,128)(2,1)S(1)}, bf16[2048,512]{1,0:T(8,128)(2,1)}, u32[]{:S(2)}) copy-start(bf16[2048,512]{1,0:T(8,128)(2,1)} %ints.3) | copy-start | bytes 6291460
  2.6 58.1 %collective-permute-start = (bf16[1024,512]{1,0:T(8,128)(2,1)}, bf16[1024,512]{1,0:T(8,128)(2,1)S(1)}, u32[]{:S(2)}, u32[]{:S(2)}) collective-permute-start(bf16[1024,512]{1,0:T(8,128)(2,1)} %get-tuple-element.14), channel_id=1, source_target_pairs={{0,512},{32,544},{64,576},{96,608},{128,640},{160,672},{192,704},{... | collective-permute-start | bytes 3145736 | tf_op jit(solution)/shard_map/ppermute | solution.py:179
  64.5 4.6 %collective-permute-start.1 = (f32[16,32,512]{2,1,0:T(8,128)S(1)}, f32[16,32,512]{2,1,0:T(8,128)S(1)}, u32[]{:S(2)}, u32[]{:S(2)}) collective-permute-start(f32[16,32,512]{2,1,0:T(8,128)S(1)} %get-tuple-element.16), channel_id=1, source_target_pairs={{0,1},{1,0},{2,3},{3,2},{4,5},{5,4},{6,7},{7,6},{8,9},{9,8},{10,11... | collective-permute-start | bytes 3145736 | tf_op jit(solution)/shard_map/ppermute | solution.py:200
  66.4 5.6 %collective-permute-start.3 = (f32[16,32,512]{2,1,0:T(8,128)S(1)}, f32[16,32,512]{2,1,0:T(8,128)S(1)}, u32[]{:S(2)}, u32[]{:S(2)}) collective-permute-start(f32[16,32,512]{2,1,0:T(8,128)S(1)} %get-tuple-element.18), channel_id=1, source_target_pairs={{0,1},{1,0},{2,3},{3,2},{4,5},{5,4},{6,7},{7,6},{8,9},{9,8},{10,11... | collective-permute-start | bytes 3145736 | tf_op jit(solution)/shard_map/ppermute | solution.py:201
  69.3 12.6 %collective-permute-start.2 = (s16[1040,128]{1,0:T(8,128)(2,1)S(1)}, s16[1040,128]{1,0:T(8,128)(2,1)S(1)}, u32[]{:S(2)}, u32[]{:S(2)}) collective-permute-start(s16[1040,128]{1,0:T(8,128)(2,1)S(1)} %shard_map.48.near), channel_id=1, source_target_pairs={{0,16},{1,17},{2,18},{3,19},{4,20},{5,21},{6,22},{7,23},{8,24},{9,... | collective-permute-start | bytes 798728 | tf_op jit(solution)/shard_map/ppermute | solution.py:223
  72.5 12.8 %collective-permute-start.4 = (s16[1040,128]{1,0:T(8,128)(2,1)S(1)}, s16[1040,128]{1,0:T(8,128)(2,1)S(1)}, u32[]{:S(2)}, u32[]{:S(2)}) collective-permute-start(s16[1040,128]{1,0:T(8,128)(2,1)S(1)} %get-tuple-element.19), channel_id=1, source_target_pairs={{0,512},{32,544},{64,576},{96,608},{128,640},{160,672},{192,704},{... | collective-permute-start | bytes 798728 | tf_op jit(solution)/shard_map/ppermute | solution.py:224
  75.5 11.3 %collective-permute-start.5 = (s16[1040,128]{1,0:T(8,128)(2,1)S(1)}, s16[1040,128]{1,0:T(8,128)(2,1)S(1)}, u32[]{:S(2)}, u32[]{:S(2)}) collective-permute-start(s16[1040,128]{1,0:T(8,128)(2,1)S(1)} %get-tuple-element.20), channel_id=1, source_target_pairs={{0,528},{1,529},{2,530},{3,531},{4,532},{5,533},{6,534},{7,535},{8... | collective-permute-start | bytes 798728 | tf_op jit(solution)/shard_map/ppermute | solution.py:225

commit v5 on v4

--- a/solution.py
+++ b/solution.py
@@ -135,7 +135,7 @@
         total = mine[half, i] + theirs[half, i]
         for came in (near, low, far):
             total += unpack(came, i, parts)
-        pack([total], shares.at[i])
+        pack([total], shares.at[Y - 1 - i])
 
 
 def last_body(shares, out):
@@ -232,7 +232,7 @@
         out_shape=jax.ShapeDtypeStruct((Y, parts * ROWS + 16, LANES), jnp.int16),
         compiler_params=pltpu.CompilerParams(vmem_limit_bytes=VMEM),
     )(place, mine, theirs, near, low, far)
-    along = [[g * CHIPS + 2 * y + c for y in range(Y)] for g in range(2) for c in range(2)]
+    along = [[g * CHIPS + 2 * y + c for y in reversed(range(Y))] for g in range(2) for c in range(2)]
     shares = lax.all_to_all(shares, "rep", 0, 0, tiled=True, axis_index_groups=along)
 
     return pl.pallas_call(

time: 108 us -> 106 us (0.981)
  blocking collectives: 74.2 us -> 71.9 us
    all_to_all x1, blocking collectives: 19.4 us -> 17 us  [per_device(): lax.all_to_all(shares, 'rep', 0, 0, tiled=True, axis_index_groups=along)]
where the time goes in v5:
time: 106 us; the launch traced here: 105 us
  blocking collectives  71.9 us (68%)
  starting transfers between devices  17.4 us (16%)
  Pallas kernels  8.34 us (8%)
  waiting for transfers between devices  7.48 us (7%)
    all_gather x1, blocking collectives, per_device(): lax.all_gather(codes[None], 'blk', axis=0, tiled=True, axis_index_groups=...  54.9 us
    all_to_all x1, blocking collectives, per_device(): lax.all_to_all(shares, 'rep', 0, 0, tiled=True, axis_index_groups=along)  17 us
    ppermute x1, starting transfers between devices, per_device(): lax.ppermute(far, ('blk', 'rep'), [(b * n + r, (b ^ Z) * n + (r ^ CHIPS))...  4.06 us
    pallas_call x1, Pallas kernels, per_device(): pl.pallas_call(product_body, in_specs=[scalar] + [inside] * 4, out_specs=...  3.82 us
    ppermute x1, waiting for transfers between devices, per_device(): low = lax.ppermute(low, 'blk', [(b, b ^ Z) for b in range(2 * Z)])  3.31 us
    ppermute x1, starting transfers between devices, per_device(): swapped = lax.ppermute(away, 'blk', [(b, b ^ Z) for b in range(2 * Z)])  3.23 us
    ppermute x1, starting transfers between devices, per_device(): low = lax.ppermute(low, 'blk', [(b, b ^ Z) for b in range(2 * Z)])  3.05 us
    ppermute x1, starting transfers between devices, per_device(): near = lax.ppermute(near, 'rep', [(r, r ^ CHIPS) for r in range(n)])  2.71 us
  transfers between devices with their start and end apart: 6, of which 4 were waited for; matrix products, arithmetic and copies ran while one was open for 0% of the time, Pallas kernels for 1%

profile of v5, /device:TPU:4, one launch (start us, length us, event | category | flops | bytes accessed | tf_op | source)
XLA Modules:
  0.0 105.2 jit_solution(18401916099709387210)
XLA Ops:
  0.0 0.0 copy-start.1
  0.0 2.6 %shard_map.46 = (s16[64,1024]{1,0:T(8,128)(2,1)}, bf16[1024,512]{1,0:T(8,128)(2,1)}) custom-call(s32[1]{0:T(128)} %bitcast.place, bf16[64,1024]{1,0:T(8,128)(2,1)} %bitcast.16, s32[1,1024]{1,0:T(1,128)} %bitcast.17, bf16[2048,512]{1,0:T(8,128)(2,1)} %ints.3, s32[8,32]{1,0:T(8,128)} %bitcast.14), custom_call_target="tpu_custom_call" | custom-call | flops 4000000 | bytes 3145728 | tf_op jit(solution)/shard_map/pallas_call | solution.py:157
  2.6 0.0 copy-start
  2.6 3.2 %collective-permute-start = (bf16[1024,512]{1,0:T(8,128)(2,1)}, bf16[1024,512]{1,0:T(8,128)(2,1)S(1)}, u32[]{:S(2)}, u32[]{:S(2)}) collective-permute-start(bf16[1024,512]{1,0:T(8,128)(2,1)} %get-tuple-element.14), channel_id=1, source_target_pairs={{0,512},{32,544},{64,576},{96,608},{128,640},{160,672},{192,704},{... | collective-permute-start | bytes 3145736 | tf_op jit(solution)/shard_map/ppermute | solution.py:179
  5.8 54.9 %all-gather.2.codes = s16[1024,1024]{1,0:T(8,128)(2,1)S(1)} all-gather(s16[64,1024]{1,0:T(8,128)(2,1)} %get-tuple-element.13), channel_id=2, replica_groups={{480,448,416,384,352,320,288,256,224,192,160,128,96,64,32,0},{992,960,9..., dimensions={0}, use_global_device_ids=true | all-gather | bytes 2228224 | tf_op jit(solution)/shard_map/all_gather | solution.py:182
  60.7 0.0 collective-permute-done.swapped
  60.7 0.0 copy-done.1
  60.7 0.0 copy-done
  60.7 3.8 %shard_map.47 = (f32[16,32,512]{2,1,0:T(8,128)S(1)}, f32[16,32,512]{2,1,0:T(8,128)S(1)}, f32[16,32,512]{2,1,0:T(8,128)S(1)}, f32[16,32,512]{2,1,0:T(8,128)S(1)}) custom-call(s32[1]{0:T(128)} %bitcast.place, s16[1024,1024]{1,0:T(8,128)(2,1)S(1)} %all-gather.2.codes, bf16[2048,512]{1,0:T(8,128)(2,1)S(1)} %copy-done, s32[8,32]{1,0:T(8,128)S(1)} %bitcast.15, ...), custom_call_target="tpu_custom_call" | custom-call | flops 2147483648 | bytes 8388608 | tf_op jit(solution)/shard_map/pallas_call | solution.py:188
  64.5 1.9 %collective-permute-start.1 = (f32[16,32,512]{2,1,0:T(8,128)S(1)}, f32[16,32,512]{2,1,0:T(8,128)S(1)}, u32[]{:S(2)}, u32[]{:S(2)}) collective-permute-start(f32[16,32,512]{2,1,0:T(8,128)S(1)} %get-tuple-element.16), channel_id=1, source_target_pairs={{0,1},{1,0},{2,3},{3,2},{4,5},{5,4},{6,7},{7,6},{8,9},{9,8},{10,11... | collective-permute-start | bytes 3145736 | tf_op jit(solution)/shard_map/ppermute | solution.py:200
  66.4 2.4 %collective-permute-start.3 = (f32[16,32,512]{2,1,0:T(8,128)S(1)}, f32[16,32,512]{2,1,0:T(8,128)S(1)}, u32[]{:S(2)}, u32[]{:S(2)}) collective-permute-start(f32[16,32,512]{2,1,0:T(8,128)S(1)} %get-tuple-element.18), channel_id=1, source_target_pairs={{0,1},{1,0},{2,3},{3,2},{4,5},{5,4},{6,7},{7,6},{8,9},{9,8},{10,11... | collective-permute-start | bytes 3145736 | tf_op jit(solution)/shard_map/ppermute | solution.py:201
  68.9 0.2 collective-permute-done.1
  69.1 0.2 shard_map.48.near
  69.3 2.7 %collective-permute-start.2 = (s16[1040,128]{1,0:T(8,128)(2,1)S(1)}, s16[1040,128]{1,0:T(8,128)(2,1)S(1)}, u32[]{:S(2)}, u32[]{:S(2)}) collective-permute-start(s16[1040,128]{1,0:T(8,128)(2,1)S(1)} %shard_map.48.near), channel_id=1, source_target_pairs={{0,16},{1,17},{2,18},{3,19},{4,20},{5,21},{6,22},{7,23},{8,24},{9,... | collective-permute-start | bytes 798728 | tf_op jit(solution)/shard_map/ppermute | solution.py:223
  72.0 0.0 collective-permute-done.3
  72.0 0.4 shard_map.49
  72.5 3.1 %collective-permute-start.4 = (s16[1040,128]{1,0:T(8,128)(2,1)S(1)}, s16[1040,128]{1,0:T(8,128)(2,1)S(1)}, u32[]{:S(2)}, u32[]{:S(2)}) collective-permute-start(s16[1040,128]{1,0:T(8,128)(2,1)S(1)} %get-tuple-element.19), channel_id=1, source_target_pairs={{0,512},{32,544},{64,576},{96,608},{128,640},{160,672},{192,704},{... | collective-permute-start | bytes 798728 | tf_op jit(solution)/shard_map/ppermute | solution.py:224
  75.5 4.1 %collective-permute-start.5 = (s16[1040,128]{1,0:T(8,128)(2,1)S(1)}, s16[1040,128]{1,0:T(8,128)(2,1)S(1)}, u32[]{:S(2)}, u32[]{:S(2)}) collective-permute-start(s16[1040,128]{1,0:T(8,128)(2,1)S(1)} %get-tuple-element.20), channel_id=1, source_target_pairs={{0,528},{1,529},{2,530},{3,531},{4,532},{5,533},{6,534},{7,535},{8... | collective-permute-start | bytes 798728 | tf_op jit(solution)/shard_map/ppermute | solution.py:225
  79.6 2.4 %collective-permute-done.2.near = s16[1040,128]{1,0:T(8,128)(2,1)S(1)} collective-permute-done((s16[1040,128]{1,0:T(8,128)(2,1)S(1)}, s16[1040,128]{1,0:T(8,128)(2,1)S(1)}, u32[]{:S(2)}, u32[]{:S(2)}) %collective-permute-start.2) | collective-permute-done | bytes 266272 | tf_op jit(solution)/shard_map/ppermute | solution.py:223
  81.9 3.3 %collective-permute-done.4.low = s16[1040,128]{1,0:T(8,128)(2,1)S(1)} collective-permute-done((s16[1040,128]{1,0:T(8,128)(2,1)S(1)}, s16[1040,128]{1,0:T(8,128)(2,1)S(1)}, u32[]{:S(2)}, u32[]{:S(2)}) %collective-permute-start.4) | collective-permute-done | bytes 266272 | tf_op jit(solution)/shard_map/ppermute | solution.py:224
  85.3 1.6 %collective-permute-done.5.far = s16[1040,128]{1,0:T(8,128)(2,1)S(1)} collective-permute-done((s16[1040,128]{1,0:T(8,128)(2,1)S(1)}, s16[1040,128]{1,0:T(8,128)(2,1)S(1)}, u32[]{:S(2)}, u32[]{:S(2)}) %collective-permute-start.5) | collective-permute-done | bytes 266272 | tf_op jit(solution)/shard_map/ppermute | solution.py:225
  86.9 0.5 shard_map.50
  87.4 17.0 %all_to_all.5.shares = s16[8,144,128]{2,1,0:T(8,128)(2,1)S(1)} all-to-all(s16[8,144,128]{2,1,0:T(8,128)(2,1)S(1)} %shard_map.50), channel_id=1, replica_groups={{14,12,10,8,6,4,2,0},{15,13,11,9,7,5,3,1},{30,28,26,24,22,20,18,16},{31..., dimensions={0} | all-to-all | bytes 589824 | tf_op jit(solution)/shard_map/all_to_all | solution.py:236
  104.4 0.8 shard_map.51
Async XLA Ops:
  0.0 60.7 %copy-start.1 = (s32[32,8]{0,1:T(8,128)S(1)}, s32[32,8]{0,1:T(8,128)}, u32[]{:S(2)}) copy-start(s32[32,8]{0,1:T(8,128)} %param.7) | copy-start | bytes 3076
  2.6 58.1 %copy-start = (bf16[2048,512]{1,0:T(8,128)(2,1)S(1)}, bf16[2048,512]{1,0:T(8,128)(2,1)}, u32[]{:S(2)}) copy-start(bf16[2048,512]{1,0:T(8,128)(2,1)} %ints.3) | copy-start | bytes 6291460
  2.6 58.1 %collective-permute-start = (bf16[1024,512]{1,0:T(8,128)(2,1)}, bf16[1024,512]{1,0:T(8,128)(2,1)S(1)}, u32[]{:S(2)}, u32[]{:S(2)}) collective-permute-start(bf16[1024,512]{1,0:T(8,128)(2,1)} %get-tuple-element.14), channel_id=1, source_target_pairs={{0,512},{32,544},{64,576},{96,608},{128,640},{160,672},{192,704},{... | collective-permute-start | bytes 3145736 | tf_op jit(solution)/shard_map/ppermute | solution.py:179
  64.5 4.6 %collective-permute-start.1 = (f32[16,32,512]{2,1,0:T(8,128)S(1)}, f32[16,32,512]{2,1,0:T(8,128)S(1)}, u32[]{:S(2)}, u32[]{:S(2)}) collective-permute-start(f32[16,32,512]{2,1,0:T(8,128)S(1)} %get-tuple-element.16), channel_id=1, source_target_pairs={{0,1},{1,0},{2,3},{3,2},{4,5},{5,4},{6,7},{7,6},{8,9},{9,8},{10,11... | collective-permute-start | bytes 3145736 | tf_op jit(solution)/shard_map/ppermute | solution.py:200
  66.4 5.6 %collective-permute-start.3 = (f32[16,32,512]{2,1,0:T(8,128)S(1)}, f32[16,32,512]{2,1,0:T(8,128)S(1)}, u32[]{:S(2)}, u32[]{:S(2)}) collective-permute-start(f32[16,32,512]{2,1,0:T(8,128)S(1)} %get-tuple-element.18), channel_id=1, source_target_pairs={{0,1},{1,0},{2,3},{3,2},{4,5},{5,4},{6,7},{7,6},{8,9},{9,8},{10,11... | collective-permute-start | bytes 3145736 | tf_op jit(solution)/shard_map/ppermute | solution.py:201
  69.3 12.6 %collective-permute-start.2 = (s16[1040,128]{1,0:T(8,128)(2,1)S(1)}, s16[1040,128]{1,0:T(8,128)(2,1)S(1)}, u32[]{:S(2)}, u32[]{:S(2)}) collective-permute-start(s16[1040,128]{1,0:T(8,128)(2,1)S(1)} %shard_map.48.near), channel_id=1, source_target_pairs={{0,16},{1,17},{2,18},{3,19},{4,20},{5,21},{6,22},{7,23},{8,24},{9,... | collective-permute-start | bytes 798728 | tf_op jit(solution)/shard_map/ppermute | solution.py:223
  72.5 12.8 %collective-permute-start.4 = (s16[1040,128]{1,0:T(8,128)(2,1)S(1)}, s16[1040,128]{1,0:T(8,128)(2,1)S(1)}, u32[]{:S(2)}, u32[]{:S(2)}) collective-permute-start(s16[1040,128]{1,0:T(8,128)(2,1)S(1)} %get-tuple-element.19), channel_id=1, source_target_pairs={{0,512},{32,544},{64,576},{96,608},{128,640},{160,672},{192,704},{... | collective-permute-start | bytes 798728 | tf_op jit(solution)/shard_map/ppermute | solution.py:224
  75.5 11.3 %collective-permute-start.5 = (s16[1040,128]{1,0:T(8,128)(2,1)S(1)}, s16[1040,128]{1,0:T(8,128)(2,1)S(1)}, u32[]{:S(2)}, u32[]{:S(2)}) collective-permute-start(s16[1040,128]{1,0:T(8,128)(2,1)S(1)} %get-tuple-element.20), channel_id=1, source_target_pairs={{0,528},{1,529},{2,530},{3,531},{4,532},{5,533},{6,534},{7,535},{8... | collective-permute-start | bytes 798728 | tf_op jit(solution)/shard_map/ppermute | solution.py:225
